TPU v7x, 128 devices: a whole 4x4x4 slice. The times are simulated.
128 devices in a mesh: row: 8 (over x_lo, y), col: 16 (over z, x_hi, core).
Axes of the slice: x: 4 (x_hi: 2, x_lo: 2; x = x_hi * 2 + x_lo), y: 4, z: 4, core: 2. Of those that a mesh axis runs over, the one named last changes fastest.
Arguments:
- cells: bfloat16 [512, 512, 256], P('row', 'col'), may hold values from -20 to 20
- row_gain: float32 [256], replicated, may hold values from 0.1 to 1.9
- row_qk: bfloat16 [256, 512], replicated, may hold values from -30 to 30
- row_value: bfloat16 [256, 256], replicated, may hold values from -0.375 to 0.375
- row_out: bfloat16 [256, 256], replicated, may hold values from -0.375 to 0.375
- col_gain: float32 [256], replicated, may hold values from 0.1 to 1.9
- col_qk: bfloat16 [256, 512], replicated, may hold values from -30 to 30
- col_value: bfloat16 [256, 256], replicated, may hold values from -0.375 to 0.375
- col_out: bfloat16 [256, 256], replicated, may hold values from -0.375 to 0.375
- mlp_gain: float32 [256], replicated, may hold values from 0.1 to 1.9
- mlp_in: bfloat16 [256, 1024], replicated, may hold values from -0.375 to 0.375
- mlp_out: bfloat16 [1024, 256], replicated, may hold values from -0.1875 to 0.1875
Outputs:
- result: bfloat16 [512, 512, 256], P('row', 'col')
All inputs are finite; a program needn't handle non-finite values.
Results may differ from a plain program's by a relative error of at most 0.012.
Values may be sent and summed in bfloat16 or wider, within the bound.
No kernel may reach another device: no remote copies, remote signals or barrier semaphores. Data moves between devices by JAX's collectives and lax.ppermute only.
A program may use at most 64 MiB of HBM per device.

v0:
```python
import math

import jax
import jax.numpy as jnp
from jax import lax
from jax.sharding import PartitionSpec as P

HEADS = 8


def layer_norm(values, gain):
    mean = jnp.mean(values, axis=-1, keepdims=True)
    centred = values - mean
    variance = jnp.mean(centred * centred, axis=-1, keepdims=True)
    return centred * lax.rsqrt(variance + 1e-05) * gain


def attend_one(line, gain, qk_w, val_w, out_w):
    length = line.shape[0]
    width = line.shape[1]
    head_size = width // HEADS
    normed = layer_norm(line.astype(jnp.float32), gain).astype(jnp.bfloat16)
    both = jnp.dot(normed, qk_w, preferred_element_type=jnp.float32).astype(jnp.bfloat16)
    values = jnp.dot(normed, val_w, preferred_element_type=jnp.float32).astype(jnp.bfloat16)
    query = both[:, :width].reshape(length, HEADS, head_size)
    keys = both[:, width:].reshape(length, HEADS, head_size)
    vals = values.reshape(length, HEADS, head_size)
    scores = jnp.einsum(
        "qhd,khd->hqk", query, keys, preferred_element_type=jnp.float32
    ) / math.sqrt(head_size)
    prob = jax.nn.softmax(scores, axis=-1).astype(jnp.bfloat16)
    mixed = (
        jnp.einsum("hqk,khd->qhd", prob, vals, preferred_element_type=jnp.float32)
        .astype(jnp.bfloat16)
        .reshape(length, width)
    )
    summed = line.astype(jnp.float32) + jnp.dot(mixed, out_w, preferred_element_type=jnp.float32)
    return summed.astype(jnp.bfloat16)


def attend_lines(lines, gain, qk_w, val_w, out_w):
    return lax.map(lambda line: attend_one(line, gain, qk_w, val_w, out_w), lines)


def per_device(
    cells,
    row_gain,
    row_qk,
    row_value,
    row_out,
    col_gain,
    col_qk,
    col_value,
    col_out,
    mlp_gain,
    mlp_in,
    mlp_out,
):
    n_row = lax.axis_size("row")
    n_col = lax.axis_size("col")
    width = cells.shape[2]
    strips = lax.all_to_all(cells, "col", split_axis=0, concat_axis=1, tiled=True)
    after_rows = attend_lines(strips, row_gain, row_qk, row_value, row_out)
    line_rows = after_rows.shape[0]
    full_cols = after_rows.shape[1]
    sub_cols = full_cols // (n_row * n_col)
    reordered = jnp.swapaxes(
        after_rows.reshape(line_rows, n_col, n_row, sub_cols, width), 1, 2
    ).reshape(line_rows, full_cols, width)
    columns = lax.all_to_all(reordered, ("row", "col"), split_axis=1, concat_axis=0, tiled=True)
    turned = jnp.swapaxes(columns, 0, 1)
    after_cols = jnp.swapaxes(attend_lines(turned, col_gain, col_qk, col_value, col_out), 0, 1)
    flat = after_cols.reshape(-1, width)
    normed = layer_norm(flat.astype(jnp.float32), mlp_gain).astype(jnp.bfloat16)
    hidden = jax.nn.gelu(
        jnp.dot(normed, mlp_in, preferred_element_type=jnp.float32), approximate=True
    ).astype(jnp.bfloat16)
    finished = (
        flat.astype(jnp.float32) + jnp.dot(hidden, mlp_out, preferred_element_type=jnp.float32)
    ).astype(jnp.bfloat16)
    finished = finished.reshape(after_cols.shape)
    return lax.all_to_all(finished, "row", split_axis=0, concat_axis=1, tiled=True)


def solution(mesh):
    in_specs = (P("row", "col", None), P(), P(), P(), P(), P(), P(), P(), P(), P(), P(), P())
    out_specs = P("row", "col", None)
    return jax.shard_map(
        per_device, mesh=mesh, in_specs=in_specs, out_specs=out_specs, check_vma=False
    )
```

profile of v0, /device:TPU:0, one launch (start us, length us, event | category | flops | bytes accessed | tf_op | source)
XLA Modules:
  0.0 185.8 jit_solution(11676150175896179648)
XLA Ops:
  0.0 8.1 %all-to-all-start = ((bf16[64,32,256]{2,1,0:T(8,128)(2,1)}), bf16[64,32,256]{2,1,0:T(8,128)(2,1)S(1)}, u32[]{:S(2)}, u32[]{:S(2)}) async-start(bf16[64,32,256]{2,1,0:T(8,128)(2,1)} %param.16), calls=%async_computation | async-start | bytes 2097152 | tf_op jit(solution)/shard_map/all_to_all | solution.py:62
  8.1 18.0 %all-to-all-done = bf16[64,32,256]{2,1,0:T(8,128)(2,1)S(1)} async-done(((bf16[64,32,256]{2,1,0:T(8,128)(2,1)}), bf16[64,32,256]{2,1,0:T(8,128)(2,1)S(1)}, u32[]{:S(2)}, u32[]{:S(2)}) %all-to-all-start) | async-done | bytes 1048608 | tf_op jit(solution)/shard_map/all_to_all | solution.py:62
  27.3 50.7 %while.20 = (s32[]{:T(128)}, bf16[4,512,256]{2,1,0:T(8,128)(2,1)}, bf16[4,512,256]{2,1,0:T(8,128)(2,1)S(1)}, f32[256]{0:T(256)}, bf16[256,256]{1,0:T(8,128)(2,1)...) while((s32[]{:T(128)}, bf16[4,512,256]{2,1,0:T(8,128)(2,1)}, ...), condition=%wide.region_5.6_spmd, body=%wide.region_0.5_spmd.sunk | while | flops 550372352 | bytes 23130808 | solution.py:42
  27.7 1.5 convolution_convert_fusion.9
  29.2 5.1 %fusion.134 = (f32[8,512]{1,0:T(8,128)S(1)}, f32[8,512,512]{1,2,0:T(8,128)}) fusion(bf16[512,8,32]{0,2,1:T(8,128)(2,1)S(1)} %bitcast.165, bf16[512,8,32]{0,2,1:T(8,128)(2,1)S(1)} %bitcast.164), kind=kOutput, calls=%fused_computation.80.clone.1 | convolution fusion | flops 140509696 | bytes 8929280 | tf_op jit(solution)/shard_map/while/body/eval_jaxpr/sub | solution.py:31
  34.7 4.3 %fusion.135 = bf16[8,32,512]{2,1,0:T(8,128)(2,1)S(1)} fusion(bf16[512,8,32]{0,2,1:T(8,128)(2,1)S(1)} %bitcast.174, f32[8,512,512]{1,2,0:T(8,128)} %get-tuple-element.220, f32[8,512]{1,0:T(8,128)S(1)} %get-tuple-element.221), kind=kOutput, calls=%fused_computation.11.clone.1 | convolution fusion | flops 138543104 | bytes 8929280 | tf_op jit(solution)/shard_map/while/body/eval_jaxpr/hqk,khd->qhd/dot_general | solution.py:33
  40.3 1.5 convolution_convert_fusion.9
  41.8 5.1 %fusion.134 = (f32[8,512]{1,0:T(8,128)S(1)}, f32[8,512,512]{1,2,0:T(8,128)}) fusion(bf16[512,8,32]{0,2,1:T(8,128)(2,1)S(1)} %bitcast.165, bf16[512,8,32]{0,2,1:T(8,128)(2,1)S(1)} %bitcast.164), kind=kOutput, calls=%fused_computation.80.clone.1 | convolution fusion | flops 140509696 | bytes 8929280 | tf_op jit(solution)/shard_map/while/body/eval_jaxpr/sub | solution.py:31
  47.3 4.3 %fusion.135 = bf16[8,32,512]{2,1,0:T(8,128)(2,1)S(1)} fusion(bf16[512,8,32]{0,2,1:T(8,128)(2,1)S(1)} %bitcast.174, f32[8,512,512]{1,2,0:T(8,128)} %get-tuple-element.220, f32[8,512]{1,0:T(8,128)S(1)} %get-tuple-element.221), kind=kOutput, calls=%fused_computation.11.clone.1 | convolution fusion | flops 138543104 | bytes 8929280 | tf_op jit(solution)/shard_map/while/body/eval_jaxpr/hqk,khd->qhd/dot_general | solution.py:33
  53.0 1.5 convolution_convert_fusion.9
  54.5 5.1 %fusion.134 = (f32[8,512]{1,0:T(8,128)S(1)}, f32[8,512,512]{1,2,0:T(8,128)}) fusion(bf16[512,8,32]{0,2,1:T(8,128)(2,1)S(1)} %bitcast.165, bf16[512,8,32]{0,2,1:T(8,128)(2,1)S(1)} %bitcast.164), kind=kOutput, calls=%fused_computation.80.clone.1 | convolution fusion | flops 140509696 | bytes 8929280 | tf_op jit(solution)/shard_map/while/body/eval_jaxpr/sub | solution.py:31
  60.0 4.3 %fusion.135 = bf16[8,32,512]{2,1,0:T(8,128)(2,1)S(1)} fusion(bf16[512,8,32]{0,2,1:T(8,128)(2,1)S(1)} %bitcast.174, f32[8,512,512]{1,2,0:T(8,128)} %get-tuple-element.220, f32[8,512]{1,0:T(8,128)S(1)} %get-tuple-element.221), kind=kOutput, calls=%fused_computation.11.clone.1 | convolution fusion | flops 138543104 | bytes 8929280 | tf_op jit(solution)/shard_map/while/body/eval_jaxpr/hqk,khd->qhd/dot_general | solution.py:33
  65.7 1.5 convolution_convert_fusion.9
  67.2 5.1 %fusion.134 = (f32[8,512]{1,0:T(8,128)S(1)}, f32[8,512,512]{1,2,0:T(8,128)}) fusion(bf16[512,8,32]{0,2,1:T(8,128)(2,1)S(1)} %bitcast.165, bf16[512,8,32]{0,2,1:T(8,128)(2,1)S(1)} %bitcast.164), kind=kOutput, calls=%fused_computation.80.clone.1 | convolution fusion | flops 140509696 | bytes 8929280 | tf_op jit(solution)/shard_map/while/body/eval_jaxpr/sub | solution.py:31
  72.7 4.3 %fusion.135 = bf16[8,32,512]{2,1,0:T(8,128)(2,1)S(1)} fusion(bf16[512,8,32]{0,2,1:T(8,128)(2,1)S(1)} %bitcast.174, f32[8,512,512]{1,2,0:T(8,128)} %get-tuple-element.220, f32[8,512]{1,0:T(8,128)S(1)} %get-tuple-element.221), kind=kOutput, calls=%fused_computation.11.clone.1 | convolution fusion | flops 138543104 | bytes 8929280 | tf_op jit(solution)/shard_map/while/body/eval_jaxpr/hqk,khd->qhd/dot_general | solution.py:33
  77.9 1.4 reshape.101
  79.3 1.4 copy.37
  80.7 23.6 %all_to_all.54 = bf16[4,512,256]{2,0,1:T(4,128)(2,1)S(1)} all-to-all(bf16[4,512,256]{2,0,1:T(4,128)(2,1)S(1)} %bitcast.169), channel_id=1, replica_groups=mesh['row'=8,'col'=16] {'row','col'}, dimensions={1} | all-to-all | bytes 2097152 | tf_op jit(solution)/shard_map/all_to_all | solution.py:70
  104.9 46.4 %while.21 = (s32[]{:T(128)}, bf16[4,512,256]{2,1,0:T(8,128)(2,1)S(1)}, bf16[4,512,256]{2,1,0:T(8,128)(2,1)S(1)}, f32[256]{0:T(256)S(1)}, bf16[256,256]{1,0:T(8,1...) while((s32[]{:T(128)}, bf16[4,512,256]{2,1,0:T(8,128)(2,1)S(1)}, ...), condition=%wide.region_11.12_spmd, body=%wide.region_6.11_spmd.sunk | while | flops 550372352 | bytes 22601860 | solution.py:42
  105.9 5.6 %fusion.148 = (f32[8,512]{1,0:T(8,128)}, f32[8,512,512]{1,2,0:T(8,128)}) fusion(bf16[512,8,32]{0,2,1:T(8,128)(2,1)S(1)} %bitcast.167, bf16[512,8,32]{0,2,1:T(8,128)(2,1)S(1)} %bitcast.166), kind=kOutput, calls=%fused_computation.82.clone.1 | convolution fusion | flops 140509696 | bytes 8929280 | tf_op jit(solution)/shard_map/while/body/eval_jaxpr/sub | solution.py:31
  112.0 4.2 %fusion.149 = bf16[8,32,512]{2,1,0:T(8,128)(2,1)S(1)} fusion(bf16[512,8,32]{0,2,1:T(8,128)(2,1)S(1)} %bitcast.176, f32[8,512,512]{1,2,0:T(8,128)} %get-tuple-element.231, f32[8,512]{1,0:T(8,128)} %get-tuple-element.232), kind=kOutput, calls=%fused_computation.37.clone.1 | convolution fusion | flops 138543104 | bytes 8929280 | tf_op jit(solution)/shard_map/while/body/eval_jaxpr/hqk,khd->qhd/dot_general | solution.py:33
  117.5 5.6 %fusion.148 = (f32[8,512]{1,0:T(8,128)}, f32[8,512,512]{1,2,0:T(8,128)}) fusion(bf16[512,8,32]{0,2,1:T(8,128)(2,1)S(1)} %bitcast.167, bf16[512,8,32]{0,2,1:T(8,128)(2,1)S(1)} %bitcast.166), kind=kOutput, calls=%fused_computation.82.clone.1 | convolution fusion | flops 140509696 | bytes 8929280 | tf_op jit(solution)/shard_map/while/body/eval_jaxpr/sub | solution.py:31
  123.6 4.2 %fusion.149 = bf16[8,32,512]{2,1,0:T(8,128)(2,1)S(1)} fusion(bf16[512,8,32]{0,2,1:T(8,128)(2,1)S(1)} %bitcast.176, f32[8,512,512]{1,2,0:T(8,128)} %get-tuple-element.231, f32[8,512]{1,0:T(8,128)} %get-tuple-element.232), kind=kOutput, calls=%fused_computation.37.clone.1 | convolution fusion | flops 138543104 | bytes 8929280 | tf_op jit(solution)/shard_map/while/body/eval_jaxpr/hqk,khd->qhd/dot_general | solution.py:33
  129.1 5.6 %fusion.148 = (f32[8,512]{1,0:T(8,128)}, f32[8,512,512]{1,2,0:T(8,128)}) fusion(bf16[512,8,32]{0,2,1:T(8,128)(2,1)S(1)} %bitcast.167, bf16[512,8,32]{0,2,1:T(8,128)(2,1)S(1)} %bitcast.166), kind=kOutput, calls=%fused_computation.82.clone.1 | convolution fusion | flops 140509696 | bytes 8929280 | tf_op jit(solution)/shard_map/while/body/eval_jaxpr/sub | solution.py:31
  135.2 4.2 %fusion.149 = bf16[8,32,512]{2,1,0:T(8,128)(2,1)S(1)} fusion(bf16[512,8,32]{0,2,1:T(8,128)(2,1)S(1)} %bitcast.176, f32[8,512,512]{1,2,0:T(8,128)} %get-tuple-element.231, f32[8,512]{1,0:T(8,128)} %get-tuple-element.232), kind=kOutput, calls=%fused_computation.37.clone.1 | convolution fusion | flops 138543104 | bytes 8929280 | tf_op jit(solution)/shard_map/while/body/eval_jaxpr/hqk,khd->qhd/dot_general | solution.py:33
  140.7 5.6 %fusion.148 = (f32[8,512]{1,0:T(8,128)}, f32[8,512,512]{1,2,0:T(8,128)}) fusion(bf16[512,8,32]{0,2,1:T(8,128)(2,1)S(1)} %bitcast.167, bf16[512,8,32]{0,2,1:T(8,128)(2,1)S(1)} %bitcast.166), kind=kOutput, calls=%fused_computation.82.clone.1 | convolution fusion | flops 140509696 | bytes 8929280 | tf_op jit(solution)/shard_map/while/body/eval_jaxpr/sub | solution.py:31
  146.8 4.2 %fusion.149 = bf16[8,32,512]{2,1,0:T(8,128)(2,1)S(1)} fusion(bf16[512,8,32]{0,2,1:T(8,128)(2,1)S(1)} %bitcast.176, f32[8,512,512]{1,2,0:T(8,128)} %get-tuple-element.231, f32[8,512]{1,0:T(8,128)} %get-tuple-element.232), kind=kOutput, calls=%fused_computation.37.clone.1 | convolution fusion | flops 138543104 | bytes 8929280 | tf_op jit(solution)/shard_map/while/body/eval_jaxpr/hqk,khd->qhd/dot_general | solution.py:33
  152.5 1.5 convert_bitcast_fusion.2
  154.5 2.9 %copy.40 = f32[512,4,256]{2,1,0:T(4,128)S(1)} copy(f32[512,4,256]{2,0,1:T(8,128)} %convert_bitcast_fusion.2) | data formatting | bytes 4194304 | tf_op jit(solution)/shard_map/convert_element_type | solution.py:79
  157.5 1.8 reshape.104
  159.3 5.7 %fusion.57 = bf16[2048,256]{1,0:T(8,128)(2,1)S(1)} fusion(f32[2048,256]{1,0:T(8,128)} %reshape.104, bf16[1024,256]{1,0:T(8,128)(2,1)S(1)} %copy-done, bf16[256,1024]{1,0:T(8,128)(2,1)S(1)} %copy-done.4, f32[256]{0:T(256)S(1)} %copy-done.9, f32[2048]{0:T(1024)S(1)} %rsqrt.28, f32[2048]{0:T(1024)S(1)} %div.43), kind=kOutput, calls=%fused_computation.64 | convolution fusion | flops 2169503744 | bytes 4211712 | tf_op jit(solution)/shard_map/dot_general | solution.py:79
  165.3 18.9 %all_to_all.55 = bf16[512,4,256]{2,1,0:T(4,128)(2,1)S(1)} all-to-all(bf16[512,4,256]{2,1,0:T(4,128)(2,1)S(1)} %reshape.103), channel_id=1, replica_groups=mesh['row'=8,'col'=16] {'row'}, dimensions={0} | all-to-all | bytes 2097152 | tf_op jit(solution)/shard_map/all_to_all | solution.py:82
  (120 shorter events, 19.3 us)
Async XLA Ops:
  0.0 159.3 %copy-start = (bf16[1024,256]{1,0:T(8,128)(2,1)S(1)}, bf16[1024,256]{1,0:T(8,128)(2,1)}, u32[]{:S(2)}) copy-start(bf16[1024,256]{1,0:T(8,128)(2,1)} %param.27) | copy-start | bytes 1572868
  0.0 26.1 %all-to-all-start = ((bf16[64,32,256]{2,1,0:T(8,128)(2,1)}), bf16[64,32,256]{2,1,0:T(8,128)(2,1)S(1)}, u32[]{:S(2)}, u32[]{:S(2)}) async-start(bf16[64,32,256]{2,1,0:T(8,128)(2,1)} %param.16), calls=%async_computation | async-start | bytes 2097152 | tf_op jit(solution)/shard_map/all_to_all | solution.py:62
  27.3 7.0 %copy-start.2 = (f32[256]{0:T(256)S(1)}, f32[256]{0:T(256)}, u32[]{:S(2)}) copy-start(f32[256]{0:T(256)} %get-tuple-element.252) | copy-start | bytes 3076 | tf_op jit(solution)/shard_map/while
  27.3 7.0 %copy-start.5 = (bf16[256,256]{1,0:T(8,128)(2,1)S(1)}, bf16[256,256]{1,0:T(8,128)(2,1)}, u32[]{:S(2)}) copy-start(bf16[256,256]{1,0:T(8,128)(2,1)} %get-tuple-element.253) | copy-start | bytes 393220 | tf_op jit(solution)/shard_map/while
  34.7 4.3 %copy-start.6 = (bf16[256,256]{1,0:T(8,128)(2,1)S(1)}, bf16[256,256]{1,0:T(8,128)(2,1)}, u32[]{:S(2)}) copy-start(bf16[256,256]{1,0:T(8,128)(2,1)} %get-tuple-element.255) | copy-start | bytes 393220 | tf_op jit(solution)/shard_map/while
  39.9 7.0 %copy-start.2 = (f32[256]{0:T(256)S(1)}, f32[256]{0:T(256)}, u32[]{:S(2)}) copy-start(f32[256]{0:T(256)} %get-tuple-element.252) | copy-start | bytes 3076 | tf_op jit(solution)/shard_map/while
  39.9 7.0 %copy-start.5 = (bf16[256,256]{1,0:T(8,128)(2,1)S(1)}, bf16[256,256]{1,0:T(8,128)(2,1)}, u32[]{:S(2)}) copy-start(bf16[256,256]{1,0:T(8,128)(2,1)} %get-tuple-element.253) | copy-start | bytes 393220 | tf_op jit(solution)/shard_map/while
  47.3 4.3 %copy-start.6 = (bf16[256,256]{1,0:T(8,128)(2,1)S(1)}, bf16[256,256]{1,0:T(8,128)(2,1)}, u32[]{:S(2)}) copy-start(bf16[256,256]{1,0:T(8,128)(2,1)} %get-tuple-element.255) | copy-start | bytes 393220 | tf_op jit(solution)/shard_map/while
  52.6 7.0 %copy-start.2 = (f32[256]{0:T(256)S(1)}, f32[256]{0:T(256)}, u32[]{:S(2)}) copy-start(f32[256]{0:T(256)} %get-tuple-element.252) | copy-start | bytes 3076 | tf_op jit(solution)/shard_map/while
  52.6 7.0 %copy-start.5 = (bf16[256,256]{1,0:T(8,128)(2,1)S(1)}, bf16[256,256]{1,0:T(8,128)(2,1)}, u32[]{:S(2)}) copy-start(bf16[256,256]{1,0:T(8,128)(2,1)} %get-tuple-element.253) | copy-start | bytes 393220 | tf_op jit(solution)/shard_map/while
  60.0 4.3 %copy-start.6 = (bf16[256,256]{1,0:T(8,128)(2,1)S(1)}, bf16[256,256]{1,0:T(8,128)(2,1)}, u32[]{:S(2)}) copy-start(bf16[256,256]{1,0:T(8,128)(2,1)} %get-tuple-element.255) | copy-start | bytes 393220 | tf_op jit(solution)/shard_map/while
  65.3 7.0 %copy-start.2 = (f32[256]{0:T(256)S(1)}, f32[256]{0:T(256)}, u32[]{:S(2)}) copy-start(f32[256]{0:T(256)} %get-tuple-element.252) | copy-start | bytes 3076 | tf_op jit(solution)/shard_map/while
  65.3 7.0 %copy-start.5 = (bf16[256,256]{1,0:T(8,128)(2,1)S(1)}, bf16[256,256]{1,0:T(8,128)(2,1)}, u32[]{:S(2)}) copy-start(bf16[256,256]{1,0:T(8,128)(2,1)} %get-tuple-element.253) | copy-start | bytes 393220 | tf_op jit(solution)/shard_map/while
  72.7 4.3 %copy-start.6 = (bf16[256,256]{1,0:T(8,128)(2,1)S(1)}, bf16[256,256]{1,0:T(8,128)(2,1)}, u32[]{:S(2)}) copy-start(bf16[256,256]{1,0:T(8,128)(2,1)} %get-tuple-element.255) | copy-start | bytes 393220 | tf_op jit(solution)/shard_map/while
  77.9 27.0 %copy-start.1 = (bf16[256,512]{1,0:T(8,128)(2,1)S(1)}, bf16[256,512]{1,0:T(8,128)(2,1)}, u32[]{:S(2)}) copy-start(bf16[256,512]{1,0:T(8,128)(2,1)} %param.22) | copy-start | bytes 786436
  77.9 27.0 %copy-start.3 = (f32[256]{0:T(256)S(1)}, f32[256]{0:T(256)}, u32[]{:S(2)}) copy-start(f32[256]{0:T(256)} %param.21) | copy-start | bytes 3076
  77.9 27.0 %copy-start.7 = (bf16[256,256]{1,0:T(8,128)(2,1)S(1)}, bf16[256,256]{1,0:T(8,128)(2,1)}, u32[]{:S(2)}) copy-start(bf16[256,256]{1,0:T(8,128)(2,1)} %param.23) | copy-start | bytes 393220
  112.0 4.3 %copy-start.8 = (bf16[256,256]{1,0:T(8,128)(2,1)S(1)}, bf16[256,256]{1,0:T(8,128)(2,1)}, u32[]{:S(2)}) copy-start(bf16[256,256]{1,0:T(8,128)(2,1)} %get-tuple-element.279) | copy-start | bytes 393220 | tf_op jit(solution)/shard_map/while
  123.6 4.3 %copy-start.8 = (bf16[256,256]{1,0:T(8,128)(2,1)S(1)}, bf16[256,256]{1,0:T(8,128)(2,1)}, u32[]{:S(2)}) copy-start(bf16[256,256]{1,0:T(8,128)(2,1)} %get-tuple-element.279) | copy-start | bytes 393220 | tf_op jit(solution)/shard_map/while
  135.2 4.3 %copy-start.8 = (bf16[256,256]{1,0:T(8,128)(2,1)S(1)}, bf16[256,256]{1,0:T(8,128)(2,1)}, u32[]{:S(2)}) copy-start(bf16[256,256]{1,0:T(8,128)(2,1)} %get-tuple-element.279) | copy-start | bytes 393220 | tf_op jit(solution)/shard_map/while
  146.8 4.3 %copy-start.8 = (bf16[256,256]{1,0:T(8,128)(2,1)S(1)}, bf16[256,256]{1,0:T(8,128)(2,1)}, u32[]{:S(2)}) copy-start(bf16[256,256]{1,0:T(8,128)(2,1)} %get-tuple-element.279) | copy-start | bytes 393220 | tf_op jit(solution)/shard_map/while
  151.3 8.0 %copy-start.4 = (bf16[256,1024]{1,0:T(8,128)(2,1)S(1)}, bf16[256,1024]{1,0:T(8,128)(2,1)}, u32[]{:S(2)}) copy-start(bf16[256,1024]{1,0:T(8,128)(2,1)} %param.26) | copy-start | bytes 1572868
  151.3 8.0 %copy-start.9 = (f32[256]{0:T(256)S(1)}, f32[256]{0:T(256)}, u32[]{:S(2)}) copy-start(f32[256]{0:T(256)} %param.25) | copy-start | bytes 3076
where the time goes:
time: 186 us
  matrix products  98.6 us (53%)
  blocking collectives  42.5 us (23%)
  waiting for transfers between devices  18 us (10%)
  local copies, waits for them, and re-layouts  12.2 us (7%)
  starting transfers between devices  8.09 us (4%)
  other arithmetic  5.68 us (3%)
    sub x8, matrix products, attend_one(): prob = jax.nn.softmax(scores, axis=-1).astype(jnp.bfloat16)  42.8 us
    dot_general x8, matrix products, attend_one(): jnp.einsum('hqk,khd->qhd', prob, vals, preferred_element_type=jnp.float32)  34 us
    all_to_all x1, blocking collectives, per_device(): lax.all_to_all(reordered, ('row', 'col'), split_axis=1, concat_axis=0, ti...  23.6 us
    all_to_all x1, blocking collectives, per_device(): lax.all_to_all(finished, 'row', split_axis=0, concat_axis=1, tiled=True)  18.9 us
    all_to_all x1, waiting for transfers between devices, per_device(): lax.all_to_all(cells, 'col', split_axis=0, concat_axis=1, tiled=True)  18 us
    all_to_all x1, starting transfers between devices, per_device(): lax.all_to_all(cells, 'col', split_axis=0, concat_axis=1, tiled=True)  8.09 us
    dot_general x8, matrix products, attend_one(): jnp.dot(normed, qk_w, preferred_element_type=jnp.float32)  7.84 us
    dot_general x1, matrix products, per_device(): jnp.dot(hidden, mlp_out, preferred_element_type=jnp.float32)  5.66 us
  transfers between devices with their start and end apart: 1, of which 1 were waited for; matrix products, arithmetic and copies ran while one was open for 0% of the time, Pallas kernels for 0%

commit v1 on v0

v1 whole, which is shorter than its diff:
```python
import math

import jax
import jax.numpy as jnp
from jax import lax
from jax.experimental import pallas as pl
from jax.experimental.pallas import tpu as pltpu
from jax.sharding import PartitionSpec as P

HEADS = 8
HEAD = 32
WIDTH = 256
LINE = 512
LINES = 4
FF = 1024
HALF = 128
GROUPS = 2
IN_GROUP = 4
BLOCK = 256
SCALE = math.log2(math.e) / math.sqrt(HEAD)
GELU_A = math.sqrt(2.0 / math.pi)
GELU_B = GELU_A * 0.044715


def layer_norm(values, gain):
    mean = jnp.mean(values, axis=-1, keepdims=True)
    centred = values - mean
    variance = jnp.mean(centred * centred, axis=-1, keepdims=True)
    return centred * lax.rsqrt(variance + 1e-05) * gain


def matmul(left, right):
    return jnp.dot(left, right, preferred_element_type=jnp.float32)


def fill_ones(mixer):
    lane = lax.broadcasted_iota(jnp.int32, (LINE, HALF), 1) // HEAD
    for group in range(GROUPS):
        for head in range(IN_GROUP):
            ones = jnp.where(lane == head, 1.0, 0.0).astype(jnp.bfloat16)
            mixer[group, head * LINE : (head + 1) * LINE, HALF:] = ones


def attend(line, gain, qk_w, val_w, out_w, mixer, probs):
    normed = layer_norm(line, gain).astype(jnp.bfloat16)
    both = matmul(normed, qk_w)
    values = matmul(normed, val_w).astype(jnp.bfloat16)
    query = both[:, :WIDTH].astype(jnp.bfloat16).astype(jnp.float32) * SCALE
    query_hi = query.astype(jnp.bfloat16)
    query_lo = (query - query_hi.astype(jnp.float32)).astype(jnp.bfloat16)
    keys = both[:, WIDTH:].astype(jnp.bfloat16)
    lane = lax.broadcasted_iota(jnp.int32, (LINE, HALF), 1) // HEAD
    mixed = []
    for group in range(GROUPS):
        lanes = slice(group * HALF, (group + 1) * HALF)
        group_query = jnp.concatenate([query_hi[:, lanes], query_lo[:, lanes]], axis=1)
        group_keys = keys[:, lanes]
        group_values = values[:, lanes]
        zero = jnp.zeros_like(group_keys)
        for head in range(IN_GROUP):
            rows = slice(head * LINE, (head + 1) * LINE)
            head_keys = jnp.where(lane == head, group_keys, zero)
            head_keys = jnp.concatenate([head_keys, head_keys], axis=1)
            mixer[group, rows, :HALF] = jnp.where(lane == head, group_values, zero)
            for start in range(0, LINE, BLOCK):
                scores = lax.dot_general(
                    group_query[start : start + BLOCK],
                    head_keys,
                    (((1,), (1,)), ((), ())),
                    preferred_element_type=jnp.float32,
                )
                scores = scores - jnp.max(scores, axis=-1, keepdims=True)
                probs[start : start + BLOCK, rows] = jnp.exp2(scores).astype(jnp.bfloat16)
        sums = matmul(probs[...], mixer[group])
        mixed.append((sums[:, :HALF] / sums[:, HALF:]).astype(jnp.bfloat16))
    return line + matmul(jnp.concatenate(mixed, axis=1), out_w)


def row_kernel(cells, gain, qk_w, val_w, out_w, out, mixer, probs, turned):
    step = pl.program_id(0)

    @pl.when(step == 0)
    def _():
        fill_ones(mixer)

    line = cells[:, 0].reshape(LINE, WIDTH).astype(jnp.float32)
    done = attend(line, gain[...], qk_w[...], val_w[...], out_w[...], mixer, probs)
    for lanes in range(GROUPS):
        turned[lanes, pl.ds(step, LINE, stride=LINES), :] = done[:, lanes * HALF : (lanes + 1) * HALF]

    @pl.when(step == LINES - 1)
    def _():
        n_row, n_col, deep = out.shape[:3]
        for lanes in range(GROUPS):
            here = slice(lanes * HALF, (lanes + 1) * HALF)
            blocks = turned[lanes].astype(jnp.bfloat16).reshape(n_col, n_row, deep, HALF)
            for r in range(n_row):
                out[r, :, :, here] = blocks[:, r]


def col_kernel(
    cells, gain, qk_w, val_w, out_w, mlp_gain, mlp_in, mlp_out, out, mixer, probs, turned
):
    step = pl.program_id(0)

    @pl.when(step == 0)
    def _():
        fill_ones(mixer)
        for lanes in range(GROUPS):
            turned[lanes] = cells[:, lanes * HALF : (lanes + 1) * HALF].astype(jnp.float32)

    parts = LINE // LINES
    line = jnp.concatenate(
        [
            jnp.concatenate(
                [
                    turned[lanes, pl.ds(step * LINES + j, parts, stride=LINES * LINES), :]
                    for lanes in range(GROUPS)
                ],
                axis=1,
            )
            for j in range(LINES)
        ],
        axis=0,
    )
    done = attend(line, gain[...], qk_w[...], val_w[...], out_w[...], mixer, probs)
    cols = done.astype(jnp.bfloat16).astype(jnp.float32)
    normed = layer_norm(cols, mlp_gain[...]).astype(jnp.bfloat16)
    pre = matmul(normed, mlp_in[...])
    inner = jnp.tanh(pre * (GELU_A + GELU_B * (pre * pre)))
    hidden = (pre * (0.5 + 0.5 * inner)).astype(jnp.bfloat16)
    result = (cols + matmul(hidden, mlp_out[...])).astype(jnp.bfloat16)
    own = out.shape[0]
    deep = parts // own
    for j in range(LINES):
        part = result[j * parts : (j + 1) * parts].reshape(own, deep, WIDTH)
        out[:, 0, j * deep : (j + 1) * deep, :] = part


def join_kernel(blocks, out, turned):
    n_row = blocks.shape[0]
    rows, cols = out.shape[0], out.shape[1]
    deep = rows // LINES
    for lanes in range(GROUPS):
        here = slice(lanes * HALF, (lanes + 1) * HALF)
        for r in range(n_row):
            for m in range(LINES):
                for j in range(LINES):
                    turned[lanes, pl.ds(j * cols + LINES * r + m, deep, stride=LINES * cols), :] = blocks[
                        r, m, j * deep : (j + 1) * deep, here
                    ].astype(jnp.float32)
    for lanes in range(GROUPS):
        here = slice(lanes * HALF, (lanes + 1) * HALF)
        out[:, :, here] = turned[lanes].astype(jnp.bfloat16).reshape(rows, cols, HALF)


def whole(array):
    return pl.BlockSpec(array.shape, lambda step: (0,) * array.ndim)


def attend_scratch():
    return [
        pltpu.VMEM((GROUPS, IN_GROUP * LINE, WIDTH), jnp.bfloat16),
        pltpu.VMEM((LINE, IN_GROUP * LINE), jnp.bfloat16),
        pltpu.VMEM((GROUPS, LINES * LINE, HALF), jnp.float32),
    ]


def params():
    return pltpu.CompilerParams(vmem_limit_bytes=48 * 2**20)


def row_attention(strips, n_row, *weights):
    n_col, lines, cols, width = strips.shape
    shape = (n_row, n_col, LINES * LINES, width)
    return pl.pallas_call(
        row_kernel,
        grid=(lines,),
        in_specs=[pl.BlockSpec((n_col, 1, cols, width), lambda step: (0, step, 0, 0))]
        + [whole(weight) for weight in weights],
        out_specs=pl.BlockSpec(shape, lambda step: (0, 0, 0, 0)),
        out_shape=jax.ShapeDtypeStruct(shape, jnp.bfloat16),
        scratch_shapes=attend_scratch(),
        compiler_params=params(),
        name="row_attention",
    )(strips, *weights)


def col_attention(cells, n_row, *weights):
    rows = LINE // n_row
    return pl.pallas_call(
        col_kernel,
        grid=(LINES,),
        in_specs=[whole(cells)] + [whole(weight) for weight in weights],
        out_specs=pl.BlockSpec((n_row, 1, rows, WIDTH), lambda step: (0, step, 0, 0)),
        out_shape=jax.ShapeDtypeStruct((n_row, LINES, rows, WIDTH), jnp.bfloat16),
        scratch_shapes=attend_scratch(),
        compiler_params=params(),
        name="col_attention_mlp",
    )(cells, *weights)


def join(blocks, rows, cols):
    return pl.pallas_call(
        join_kernel,
        out_shape=jax.ShapeDtypeStruct((rows, cols, WIDTH), jnp.bfloat16),
        scratch_shapes=[pltpu.VMEM((GROUPS, LINES * LINE, HALF), jnp.float32)],
        compiler_params=params(),
        name="join_blocks",
    )(blocks)


def per_device(
    cells,
    row_gain,
    row_qk,
    row_value,
    row_out,
    col_gain,
    col_qk,
    col_value,
    col_out,
    mlp_gain,
    mlp_in,
    mlp_out,
):
    n_row = lax.axis_size("row")
    n_col = lax.axis_size("col")
    rows, cols, width = cells.shape
    row_gain, col_gain, mlp_gain = (g.reshape(1, width) for g in (row_gain, col_gain, mlp_gain))
    strips = lax.all_to_all(cells, "col", split_axis=0, concat_axis=0, tiled=True)
    strips = strips.reshape(n_col, rows // n_col, cols, width)
    after_rows = row_attention(strips, n_row, row_gain, row_qk, row_value, row_out)
    columns = lax.all_to_all(
        after_rows.reshape(-1, width), ("row", "col"), split_axis=0, concat_axis=0, tiled=True
    )
    finished = col_attention(
        columns, n_row, col_gain, col_qk, col_value, col_out, mlp_gain, mlp_in, mlp_out
    )
    blocks = lax.all_to_all(
        finished.reshape(-1, width), "row", split_axis=0, concat_axis=0, tiled=True
    )
    return join(blocks.reshape(n_row, LINES, rows, width), rows, cols)


def solution(mesh):
    in_specs = (P("row", "col", None), P(), P(), P(), P(), P(), P(), P(), P(), P(), P(), P())
    out_specs = P("row", "col", None)
    return jax.shard_map(
        per_device, mesh=mesh, in_specs=in_specs, out_specs=out_specs, check_vma=False
    )
```

time: 186 us -> 108 us (0.58)
  matrix products: 98.6 us -> 0 us
  Pallas kernels: 0 us -> 37.3 us
  blocking collectives: 42.5 us -> 68.5 us
  waiting for transfers between devices: 18 us -> 0 us
  local copies, waits for them, and re-layouts: 12.2 us -> 1.35 us
  starting transfers between devices: 8.09 us -> 0 us
  other arithmetic: 5.68 us -> 0 us
    dot_general x33 -> x0, matrix products: 55.9 us -> none  [the longest x8 34 us: attend_one(): jnp.einsum('hqk,khd->qhd', prob, vals, preferred_element_type=jnp.float32)]
    sub x8 -> x0, matrix products: 42.8 us -> none  [attend_one(): prob = jax.nn.softmax(scores, axis=-1).astype(jnp.bfloat16)]
    pallas_call x0 -> x3, Pallas kernels: none -> 37.3 us  [the longest x1 20.4 us: col_attention(): pl.pallas_call(col_kernel, grid=(LINES,), in_specs=[whole(cells)] + [whol...]
    all_to_all x2 -> x3, blocking collectives: 42.5 us -> 68.5 us  [the longest x1 26.1 us: per_device(): lax.all_to_all(cells, 'col', split_axis=0, concat_axis=0, tiled=True)]
    all_to_all x1 -> x0, waiting for transfers between devices: 18 us -> none  [per_device(): lax.all_to_all(cells, 'col', split_axis=0, concat_axis=1, tiled=True)]
    all_to_all x1 -> x0, starting transfers between devices: 8.09 us -> none  [per_device(): lax.all_to_all(cells, 'col', split_axis=0, concat_axis=1, tiled=True)]
    convert_element_type x2 -> x0, local copies, waits for them, and re-layouts: 4.73 us -> none  [per_device(): flat.astype(jnp.float32)]
    reduce_sum x18 -> x0, other arithmetic: 4.03 us -> none  [the longest x9 2.49 us: layer_norm(): variance = jnp.mean(centred * centred, axis=-1, keepdims=True)]
  transfers between devices with their start and end apart: 1 -> 0, of which waited for: 1 -> 0; matrix products, arithmetic and copies ran while one was open for 0% -> 0% of each run, Pallas kernels for 0% -> 0%
where the time goes in v1:
time: 108 us; the launch traced here: 107 us
  blocking collectives  68.5 us (63%)
  Pallas kernels  37.3 us (35%)
  local copies, waits for them, and re-layouts  1.35 us (1%)
    all_to_all x1, blocking collectives, per_device(): lax.all_to_all(cells, 'col', split_axis=0, concat_axis=0, tiled=True)  26.1 us
    all_to_all x1, blocking collectives, per_device(): lax.all_to_all(after_rows.reshape(-1, width), ('row', 'col'), split_axis=...  23.5 us
    pallas_call x1, Pallas kernels, col_attention(): pl.pallas_call(col_kernel, grid=(LINES,), in_specs=[whole(cells)] + [whol...  20.4 us
    all_to_all x1, blocking collectives, per_device(): lax.all_to_all(finished.reshape(-1, width), 'row', split_axis=0, concat_a...  18.9 us
    pallas_call x1, Pallas kernels, row_attention(): pl.pallas_call(row_kernel, grid=(lines,), in_specs=[pl.BlockSpec((n_col,...  13.7 us
    pallas_call x1, Pallas kernels, join(): pl.pallas_call(join_kernel, out_shape=jax.ShapeDtypeStruct((rows, cols, W...  3.18 us

profile of v1, /device:TPU:0, one launch (start us, length us, event | category | flops | bytes accessed | tf_op | source)
XLA Modules:
  0.0 107.3 jit_solution(8041717115618631033)
XLA Ops:
  0.0 0.0 copy-start.5
  0.0 0.0 copy-start.4
  0.0 0.0 copy-start.2
  0.0 26.1 %all_to_all.25 = bf16[64,32,256]{2,1,0:T(8,128)(2,1)S(1)} all-to-all(bf16[64,32,256]{2,1,0:T(8,128)(2,1)} %param.12), channel_id=1, replica_groups=mesh['row'=8,'col'=16] {'col'}, dimensions={0} | all-to-all | bytes 2097152 | tf_op jit(solution)/shard_map/all_to_all | solution.py:231
  26.1 0.0 copy-start.8
  26.1 0.0 copy-done.5
  26.1 0.0 copy-done.4
  26.1 0.0 copy-done.2
  26.1 0.7 copy-done.8
  26.8 13.7 %row_attention.1 = bf16[8,16,16,256]{3,2,1,0:T(8,128)(2,1)S(1)} custom-call(bf16[16,4,32,256]{3,2,1,0:T(8,128)(2,1)S(1)} %bitcast.11, f32[1,256]{1,0:T(1,128)S(1)} %bitcast.13, bf16[256,512]{1,0:T(8,128)(2,1)S(1)} %copy-done.2, bf16[256,256]{1,0:T(8,128)(2,1)S(1)} %copy-done.4, bf16[256,256]{1,0:T(8,128)(2,1)S(1)} %copy-done.5), custom_call_target="tpu_custom_call" | custom-call | tf_op jit(solution)/shard_map/row_attention/pallas_call | solution.py:176
  40.5 0.0 copy-start
  40.5 0.0 copy-start.1
  40.5 0.0 copy-start.3
  40.5 0.0 copy-start.6
  40.5 0.0 copy-start.7
  40.5 0.0 copy-start.10
  40.6 23.5 %all_to_all.26 = bf16[128,16,256]{2,1,0:T(8,128)(2,1)S(1)} all-to-all(bf16[128,16,256]{2,1,0:T(8,128)(2,1)S(1)} %bitcast.8), channel_id=1, replica_groups=mesh['row'=8,'col'=16] {'row','col'}, dimensions={0} | all-to-all | bytes 2097152 | tf_op jit(solution)/shard_map/all_to_all | solution.py:234
  64.1 0.0 copy-start.9
  64.1 0.0 copy-done
  64.1 0.0 copy-done.1
  64.1 0.0 copy-done.3
  64.1 0.0 copy-done.6
  64.1 0.0 copy-done.7
  64.1 0.0 copy-done.10
  64.2 0.6 copy-done.9
  64.8 20.4 %col_attention_mlp.1 = bf16[8,4,64,256]{3,2,1,0:T(8,128)(2,1)S(1)} custom-call(bf16[2048,256]{1,0:T(8,128)(2,1)S(1)} %bitcast.9, f32[1,256]{1,0:T(1,128)S(1)} %bitcast.14, bf16[256,512]{1,0:T(8,128)(2,1)S(1)} %copy-done.3, bf16[256,256]{1,0:T(8,128)(2,1)S(1)} %copy-done.6, bf16[256,256]{1,0:T(8,128)(2,1)S(1)} %copy-done.7, f32[1,256]{1,0:T(1,128)S(1)} %bitcast.15, ...), custom_call_target="tpu_custom_call" | custom-call | tf_op jit(solution)/shard_map/col_attention_mlp/pallas_call | solution.py:191
  85.2 18.9 %all_to_all.27 = bf16[8,256,256]{2,1,0:T(8,128)(2,1)S(1)} all-to-all(bf16[8,256,256]{2,1,0:T(8,128)(2,1)S(1)} %bitcast.10), channel_id=1, replica_groups=mesh['row'=8,'col'=16] {'row'}, dimensions={0} | all-to-all | bytes 2097152 | tf_op jit(solution)/shard_map/all_to_all | solution.py:240
  104.1 3.2 %join_blocks.1 = bf16[64,32,256]{2,1,0:T(8,128)(2,1)} custom-call(bf16[8,4,64,256]{3,2,1,0:T(8,128)(2,1)S(1)} %bitcast.12), custom_call_target="tpu_custom_call" | custom-call | tf_op jit(solution)/shard_map/join_blocks/pallas_call | solution.py:204
Async XLA Ops:
  0.0 26.1 %copy-start.5 = (bf16[256,256]{1,0:T(8,128)(2,1)S(1)}, bf16[256,256]{1,0:T(8,128)(2,1)}, u32[]{:S(2)}) copy-start(bf16[256,256]{1,0:T(8,128)(2,1)} %out_w.2) | copy-start | bytes 393220
  0.0 26.1 %copy-start.4 = (bf16[256,256]{1,0:T(8,128)(2,1)S(1)}, bf16[256,256]{1,0:T(8,128)(2,1)}, u32[]{:S(2)}) copy-start(bf16[256,256]{1,0:T(8,128)(2,1)} %val_w.2) | copy-start | bytes 393220
  0.0 26.1 %copy-start.2 = (bf16[256,512]{1,0:T(8,128)(2,1)S(1)}, bf16[256,512]{1,0:T(8,128)(2,1)}, u32[]{:S(2)}) copy-start(bf16[256,512]{1,0:T(8,128)(2,1)} %qk_w.2) | copy-start | bytes 786436
  26.1 0.7 copy-start.8
  40.5 23.6 %copy-start = (bf16[256,1024]{1,0:T(8,128)(2,1)S(1)}, bf16[256,1024]{1,0:T(8,128)(2,1)}, u32[]{:S(2)}) copy-start(bf16[256,1024]{1,0:T(8,128)(2,1)} %mlp_in.1) | copy-start | bytes 1572868
  40.5 23.6 %copy-start.1 = (bf16[1024,256]{1,0:T(8,128)(2,1)S(1)}, bf16[1024,256]{1,0:T(8,128)(2,1)}, u32[]{:S(2)}) copy-start(bf16[1024,256]{1,0:T(8,128)(2,1)} %mlp_out.1) | copy-start | bytes 1572868
  40.5 23.6 %copy-start.3 = (bf16[256,512]{1,0:T(8,128)(2,1)S(1)}, bf16[256,512]{1,0:T(8,128)(2,1)}, u32[]{:S(2)}) copy-start(bf16[256,512]{1,0:T(8,128)(2,1)} %qk_w.3) | copy-start | bytes 786436
  40.5 23.6 %copy-start.6 = (bf16[256,256]{1,0:T(8,128)(2,1)S(1)}, bf16[256,256]{1,0:T(8,128)(2,1)}, u32[]{:S(2)}) copy-start(bf16[256,256]{1,0:T(8,128)(2,1)} %val_w.3) | copy-start | bytes 393220
  40.5 23.6 %copy-start.7 = (bf16[256,256]{1,0:T(8,128)(2,1)S(1)}, bf16[256,256]{1,0:T(8,128)(2,1)}, u32[]{:S(2)}) copy-start(bf16[256,256]{1,0:T(8,128)(2,1)} %out_w.3) | copy-start | bytes 393220
  40.5 23.6 %copy-start.10 = (f32[256]{0:T(256)S(1)}, f32[256]{0:T(256)}, u32[]{:S(2)}) copy-start(f32[256]{0:T(256)} %param.21) | copy-start | bytes 3076
  64.1 0.7 copy-start.9

commit v2 on v0

v2 whole, which is shorter than its diff:
```python
import math

import jax
import jax.numpy as jnp
from jax import lax
from jax.experimental import pallas as pl
from jax.experimental.pallas import tpu as pltpu
from jax.sharding import PartitionSpec as P

HEADS = 8
HEAD = 32
WIDTH = 256
LINE = 512
LINES = 4
HALF = 128
GROUPS = 2
IN_GROUP = 4
BLOCK = 256
SCALE = math.log2(math.e) / math.sqrt(HEAD)
GELU_A = math.sqrt(2.0 / math.pi)
GELU_B = GELU_A * 0.044715


def layer_norm(values, gain):
    mean = jnp.mean(values, axis=-1, keepdims=True)
    centred = values - mean
    variance = jnp.mean(centred * centred, axis=-1, keepdims=True)
    return centred * lax.rsqrt(variance + 1e-05) * gain


def matmul(left, right):
    return jnp.dot(left, right, preferred_element_type=jnp.float32)


def fill_ones(mixer):
    lane = lax.broadcasted_iota(jnp.int32, (LINE, HALF), 1) // HEAD
    for group in range(GROUPS):
        for head in range(IN_GROUP):
            ones = jnp.where(lane == head, 1.0, 0.0).astype(jnp.bfloat16)
            mixer[group, head * LINE : (head + 1) * LINE, HALF:] = ones


class Line:
    def __init__(self, load, store, gain, qk_w, val_w, out_w, mixer, probs):
        self.load, self.store = load, store
        self.gain, self.qk_w, self.val_w, self.out_w = gain, qk_w, val_w, out_w
        self.mixer, self.probs = mixer, probs
        self.mixed = []

    def project(self):
        normed = layer_norm(self.load(), self.gain[...]).astype(jnp.bfloat16)
        both = matmul(normed, self.qk_w[...])
        self.values = matmul(normed, self.val_w[...]).astype(jnp.bfloat16)
        query = both[:, :WIDTH].astype(jnp.bfloat16).astype(jnp.float32) * SCALE
        self.query_hi = query.astype(jnp.bfloat16)
        self.query_lo = (query - self.query_hi.astype(jnp.float32)).astype(jnp.bfloat16)
        self.keys = both[:, WIDTH:].astype(jnp.bfloat16)

    def weigh(self, group):
        lanes = slice(group * HALF, (group + 1) * HALF)
        query = jnp.concatenate([self.query_hi[:, lanes], self.query_lo[:, lanes]], axis=1)
        keys = self.keys[:, lanes]
        values = self.values[:, lanes]
        zero = jnp.zeros_like(keys)
        lane = lax.broadcasted_iota(jnp.int32, (LINE, HALF), 1) // HEAD
        for head in range(IN_GROUP):
            rows = slice(head * LINE, (head + 1) * LINE)
            self.mixer[group, rows, :HALF] = jnp.where(lane == head, values, zero)
            head_keys = jnp.where(lane == head, keys, zero)
            head_keys = jnp.concatenate([head_keys, head_keys], axis=1)
            for start in range(0, LINE, BLOCK):
                scores = lax.dot_general(
                    query[start : start + BLOCK],
                    head_keys,
                    (((1,), (1,)), ((), ())),
                    preferred_element_type=jnp.float32,
                )
                scores = scores - jnp.max(scores, axis=-1, keepdims=True)
                self.probs[group, start : start + BLOCK, rows] = jnp.exp2(scores).astype(jnp.bfloat16)

    def mix(self, group):
        sums = matmul(self.probs[group], self.mixer[group])
        self.mixed.append((sums[:, :HALF] / sums[:, HALF:]).astype(jnp.bfloat16))

    def finish(self):
        self.store(self.load() + matmul(jnp.concatenate(self.mixed, axis=1), self.out_w[...]))


def attend(lines):
    lines[0].project()
    lines[0].weigh(0)
    for line, later in zip(lines, lines[1:] + [None]):
        line.mix(0)
        line.weigh(1)
        if later is not None:
            later.project()
        line.mix(1)
        if later is not None:
            later.weigh(0)
        line.finish()


def row_kernel(
    cells, gain, qk_w, val_w, out_w, later_gain, last_gain, out, later_out, last_out, mixer, probs, turned
):
    fill_ones(mixer)
    later_out[...] = later_gain[...]
    last_out[...] = last_gain[...]

    def line(j):
        def load():
            return cells[:, j].reshape(LINE, WIDTH).astype(jnp.float32)

        def store(done):
            for lanes in range(GROUPS):
                turned[lanes, pl.ds(j, LINE, stride=LINES), :] = done[:, lanes * HALF : (lanes + 1) * HALF]

        return Line(load, store, gain, qk_w, val_w, out_w, mixer, probs)

    attend([line(j) for j in range(LINES)])
    n_row, n_col, deep = out.shape[:3]
    for lanes in range(GROUPS):
        here = slice(lanes * HALF, (lanes + 1) * HALF)
        blocks = turned[lanes].astype(jnp.bfloat16).reshape(n_col, n_row, deep, HALF)
        for r in range(n_row):
            out[r, :, :, here] = blocks[:, r]


def col_kernel(cells, gain, qk_w, val_w, out_w, out, mixer, probs):
    fill_ones(mixer)

    def line(m):
        def load():
            tiles = cells[...].reshape(LINE // LINES, LINES * LINES, WIDTH)[:, m // 2 * 8 : m // 2 * 8 + 8]
            tiles = tiles.astype(jnp.float32).reshape(LINE // 8, 2, 8, WIDTH)
            even, odd = tiles[:, 0], tiles[:, 1]
            if m % 2:
                even = pltpu.roll(even, LINES, 1)
            else:
                odd = pltpu.roll(odd, LINES, 1)
            row = lax.broadcasted_iota(jnp.int32, even.shape, 1)
            return jnp.where(row < LINES, even, odd).reshape(LINE, WIDTH)

        def store(done):
            out[:, m] = done.astype(jnp.bfloat16).reshape(out.shape[0], out.shape[2], WIDTH)

        return Line(load, store, gain, qk_w, val_w, out_w, mixer, probs)

    attend([line(m) for m in range(LINES)])


def mlp_kernel(blocks, gain, in_w, out_w, out, swap, done, sems):
    rows, cols = out.shape[:2]
    deep = rows // LINES
    cells = deep * cols
    to = lax.broadcasted_iota(jnp.int32, (cells, cells), 0)
    come = lax.broadcasted_iota(jnp.int32, (cells, cells), 1)
    moved = come == to % cols * deep + to // cols
    swap[...] = jnp.where(moved, 1.0, 0.0).astype(jnp.bfloat16)
    copies = []
    for part in range(LINES):
        here = slice(part * deep, (part + 1) * deep)
        line = matmul(swap[...], blocks[:, :, here].reshape(cells, WIDTH))
        normed = layer_norm(line, gain[...]).astype(jnp.bfloat16)
        for start in range(0, cells, BLOCK):
            pre = matmul(normed[start : start + BLOCK], in_w[...])
            inner = jnp.tanh(pre * (GELU_A + GELU_B * (pre * pre)))
            hidden = (pre * (0.5 + 0.5 * inner)).astype(jnp.bfloat16)
            result = line[start : start + BLOCK] + matmul(hidden, out_w[...])
            first = part * deep + start // cols
            done[first : first + BLOCK // cols] = result.astype(jnp.bfloat16).reshape(
                BLOCK // cols, cols, WIDTH
            )
        copies.append(pltpu.make_async_copy(done.at[here], out.at[here], sems.at[part]))
        copies[-1].start()
    for copy in copies:
        copy.wait()


IN_VMEM = pl.BlockSpec(memory_space=pltpu.VMEM)
PARAMS = pltpu.CompilerParams(vmem_limit_bytes=40 * 2**20)


def bf16(*shape):
    return jax.ShapeDtypeStruct(shape, jnp.bfloat16)


def attend_scratch():
    return [
        pltpu.VMEM((GROUPS, IN_GROUP * LINE, WIDTH), jnp.bfloat16),
        pltpu.VMEM((GROUPS, LINE, IN_GROUP * LINE), jnp.bfloat16),
    ]


def row_attention(n_row, strips, gain, qk_w, val_w, out_w, *gains):
    n_col = strips.shape[0]
    return pl.pallas_call(
        row_kernel,
        in_specs=[IN_VMEM] * 7,
        out_specs=[IN_VMEM] * 3,
        out_shape=[bf16(n_row, n_col, LINES * LINES, WIDTH)]
        + [jax.ShapeDtypeStruct(later.shape, later.dtype) for later in gains],
        scratch_shapes=attend_scratch() + [pltpu.VMEM((GROUPS, LINES * LINE, HALF), jnp.float32)],
        compiler_params=PARAMS,
        name="row_attention",
    )(strips, gain, qk_w, val_w, out_w, *gains)


def col_attention(n_row, columns, *weights):
    return pl.pallas_call(
        col_kernel,
        in_specs=[IN_VMEM] * 5,
        out_specs=IN_VMEM,
        out_shape=bf16(n_row, LINES, LINE // n_row, WIDTH),
        scratch_shapes=attend_scratch(),
        compiler_params=PARAMS,
        name="col_attention",
    )(columns, *weights)


def mlp(cols, blocks, *weights):
    rows = blocks.shape[2]
    cells = rows // LINES * cols
    return pl.pallas_call(
        mlp_kernel,
        in_specs=[IN_VMEM] * 4,
        out_specs=pl.BlockSpec(memory_space=pl.ANY),
        out_shape=bf16(rows, cols, WIDTH),
        scratch_shapes=[
            pltpu.VMEM((cells, cells), jnp.bfloat16),
            pltpu.VMEM((rows, cols, WIDTH), jnp.bfloat16),
            pltpu.SemaphoreType.DMA((LINES,)),
        ],
        compiler_params=PARAMS,
        name="mlp",
    )(blocks, *weights)


def per_device(
    cells,
    row_gain,
    row_qk,
    row_value,
    row_out,
    col_gain,
    col_qk,
    col_value,
    col_out,
    mlp_gain,
    mlp_in,
    mlp_out,
):
    n_row = lax.axis_size("row")
    n_col = lax.axis_size("col")
    rows, cols, width = cells.shape
    row_gain, col_gain, mlp_gain = (g.reshape(1, width) for g in (row_gain, col_gain, mlp_gain))
    strips = lax.all_to_all(cells, "col", split_axis=0, concat_axis=0, tiled=True)
    strips = strips.reshape(n_col, LINES, cols, width)
    after_rows, col_gain, mlp_gain = row_attention(
        n_row, strips, row_gain, row_qk, row_value, row_out, col_gain, mlp_gain
    )
    columns = lax.all_to_all(
        after_rows.reshape(-1, width), ("row", "col"), split_axis=0, concat_axis=0, tiled=True
    )
    after_cols = col_attention(n_row, columns, col_gain, col_qk, col_value, col_out)
    blocks = lax.all_to_all(
        after_cols.reshape(-1, width), "row", split_axis=0, concat_axis=0, tiled=True
    )
    return mlp(cols, blocks.reshape(n_row, LINES, rows, width), mlp_gain, mlp_in, mlp_out)


def solution(mesh):
    in_specs = (P("row", "col", None), P(), P(), P(), P(), P(), P(), P(), P(), P(), P(), P())
    out_specs = P("row", "col", None)
    return jax.shard_map(
        per_device, mesh=mesh, in_specs=in_specs, out_specs=out_specs, check_vma=False
    )
```

time: 186 us -> 101 us (0.54)
  matrix products: 98.6 us -> 0 us
  Pallas kernels: 0 us -> 30.6 us
  blocking collectives: 42.5 us -> 68.6 us
  waiting for transfers between devices: 18 us -> 0 us
  local copies, waits for them, and re-layouts: 12.2 us -> 0.7 us
  starting transfers between devices: 8.09 us -> 0 us
  other arithmetic: 5.68 us -> 0 us
    dot_general x33 -> x0, matrix products: 55.9 us -> none  [the longest x8 34 us: attend_one(): jnp.einsum('hqk,khd->qhd', prob, vals, preferred_element_type=jnp.float32)]
    sub x8 -> x0, matrix products: 42.8 us -> none  [attend_one(): prob = jax.nn.softmax(scores, axis=-1).astype(jnp.bfloat16)]
    pallas_call x0 -> x3, Pallas kernels: none -> 30.6 us  [the longest x1 12.5 us: col_attention(): pl.pallas_call(col_kernel, in_specs=[IN_VMEM] * 5, out_specs=IN_VMEM, out...]
    all_to_all x2 -> x3, blocking collectives: 42.5 us -> 68.6 us  [the longest x1 26.1 us: per_device(): lax.all_to_all(cells, 'col', split_axis=0, concat_axis=0, tiled=True)]
    all_to_all x1 -> x0, waiting for transfers between devices: 18 us -> none  [per_device(): lax.all_to_all(cells, 'col', split_axis=0, concat_axis=1, tiled=True)]
    all_to_all x1 -> x0, starting transfers between devices: 8.09 us -> none  [per_device(): lax.all_to_all(cells, 'col', split_axis=0, concat_axis=1, tiled=True)]
    convert_element_type x2 -> x0, local copies, waits for them, and re-layouts: 4.73 us -> none  [per_device(): flat.astype(jnp.float32)]
    reduce_sum x18 -> x0, other arithmetic: 4.03 us -> none  [the longest x9 2.49 us: layer_norm(): variance = jnp.mean(centred * centred, axis=-1, keepdims=True)]
  transfers between devices with their start and end apart: 1 -> 0, of which waited for: 1 -> 0; matrix products, arithmetic and copies ran while one was open for 0% -> 0% of each run, Pallas kernels for 0% -> 0%
where the time goes in v2:
time: 101 us; the launch traced here: 100 us
  blocking collectives  68.6 us (68%)
  Pallas kernels  30.6 us (30%)
    all_to_all x1, blocking collectives, per_device(): lax.all_to_all(cells, 'col', split_axis=0, concat_axis=0, tiled=True)  26.1 us
    all_to_all x1, blocking collectives, per_device(): lax.all_to_all(after_rows.reshape(-1, width), ('row', 'col'), split_axis=...  23.5 us
    all_to_all x1, blocking collectives, per_device(): lax.all_to_all(after_cols.reshape(-1, width), 'row', split_axis=0, concat...  19 us
    pallas_call x1, Pallas kernels, col_attention(): pl.pallas_call(col_kernel, in_specs=[IN_VMEM] * 5, out_specs=IN_VMEM, out...  12.5 us
    pallas_call x1, Pallas kernels, row_attention(): pl.pallas_call(row_kernel, in_specs=[IN_VMEM] * 7, out_specs=[IN_VMEM] *...  12.5 us
    pallas_call x1, Pallas kernels, mlp(): pl.pallas_call(mlp_kernel, in_specs=[IN_VMEM] * 4, out_specs=pl.BlockSpec...  5.57 us

profile of v2, /device:TPU:0, one launch (start us, length us, event | category | flops | bytes accessed | tf_op | source)
XLA Modules:
  0.0 100.2 jit_solution(3359628407588639197)
XLA Ops:
  0.0 0.0 copy-start.7
  0.0 0.0 copy-start.6
  0.0 0.0 copy-start.3
  0.0 0.0 copy-start.9
  0.0 0.0 copy-start.10
  0.0 26.1 %all_to_all.25 = bf16[64,32,256]{2,1,0:T(8,128)(2,1)S(1)} all-to-all(bf16[64,32,256]{2,1,0:T(8,128)(2,1)} %param.12), channel_id=1, replica_groups=mesh['row'=8,'col'=16] {'col'}, dimensions={0} | all-to-all | bytes 2097152 | tf_op jit(solution)/shard_map/all_to_all | solution.py:257
  26.1 0.0 copy-start.8
  26.1 0.0 copy-done.7
  26.1 0.0 copy-done.6
  26.1 0.0 copy-done.3
  26.1 0.0 copy-done.9
  26.1 0.0 copy-done.10
  26.1 0.6 copy-done.8
  26.8 12.5 %row_attention.1 = (bf16[8,16,16,256]{3,2,1,0:T(8,128)(2,1)S(1)}, f32[1,256]{1,0:T(1,128)S(1)}, f32[1,256]{1,0:T(1,128)S(1)}) custom-call(bf16[16,4,32,256]{3,2,1,0:T(8,128)(2,1)S(1)} %bitcast.10, f32[1,256]{1,0:T(1,128)S(1)} %bitcast.13, bf16[256,512]{1,0:T(8,128)(2,1)S(1)} %copy-done.3, bf16[256,256]{1,0:T(8,128)(2,1)S(1)} %copy-done.6, ...), custom_call_target="tpu_custom_call" | custom-call | tf_op jit(solution)/shard_map/row_attention/pallas_call | solution.py:197
  39.3 0.0 copy-start.2
  39.3 0.0 copy-start.4
  39.3 0.0 copy-start.5
  39.3 23.5 %all_to_all.26 = bf16[128,16,256]{2,1,0:T(8,128)(2,1)S(1)} all-to-all(bf16[128,16,256]{2,1,0:T(8,128)(2,1)S(1)} %bitcast.12), channel_id=1, replica_groups=mesh['row'=8,'col'=16] {'row','col'}, dimensions={0} | all-to-all | bytes 2097152 | tf_op jit(solution)/shard_map/all_to_all | solution.py:262
  62.9 0.0 copy-done.2
  62.9 0.0 copy-done.4
  62.9 0.0 copy-done.5
  62.9 12.5 %col_attention.1 = bf16[8,4,64,256]{3,2,1,0:T(8,128)(2,1)S(1)} custom-call(bf16[2048,256]{1,0:T(8,128)(2,1)S(1)} %bitcast.8, f32[1,256]{1,0:T(1,128)S(1)} %get-tuple-element.9.gain, bf16[256,512]{1,0:T(8,128)(2,1)S(1)} %copy-done.2, bf16[256,256]{1,0:T(8,128)(2,1)S(1)} %copy-done.4, bf16[256,256]{1,0:T(8,128)(2,1)S(1)} %copy-done.5), custom_call_target="tpu_custom_call" | custom-call | tf_op jit(solution)/shard_map/col_attention/pallas_call | solution.py:210
  75.4 0.0 copy-start
  75.5 0.0 copy-start.1
  75.5 19.0 %all_to_all.27 = bf16[8,256,256]{2,1,0:T(8,128)(2,1)S(1)} all-to-all(bf16[8,256,256]{2,1,0:T(8,128)(2,1)S(1)} %bitcast.9), channel_id=1, replica_groups=mesh['row'=8,'col'=16] {'row'}, dimensions={0} | all-to-all | bytes 2097152 | tf_op jit(solution)/shard_map/all_to_all | solution.py:266
  94.5 0.0 copy-done
  94.5 0.0 copy-done.1
  94.5 5.6 %mlp.1 = bf16[64,32,256]{2,1,0:T(8,128)(2,1)} custom-call(bf16[8,4,64,256]{3,2,1,0:T(8,128)(2,1)S(1)} %bitcast.11, f32[1,256]{1,0:T(1,128)S(1)} %get-tuple-element.10.gain, bf16[256,1024]{1,0:T(8,128)(2,1)S(1)} %copy-done, bf16[1024,256]{1,0:T(8,128)(2,1)S(1)} %copy-done.1), custom_call_target="tpu_custom_call" | custom-call | tf_op jit(solution)/shard_map/mlp/pallas_call | solution.py:224
Async XLA Ops:
  0.0 26.1 %copy-start.7 = (bf16[256,256]{1,0:T(8,128)(2,1)S(1)}, bf16[256,256]{1,0:T(8,128)(2,1)}, u32[]{:S(2)}) copy-start(bf16[256,256]{1,0:T(8,128)(2,1)} %out_w.3) | copy-start | bytes 393220
  0.0 26.1 %copy-start.6 = (bf16[256,256]{1,0:T(8,128)(2,1)S(1)}, bf16[256,256]{1,0:T(8,128)(2,1)}, u32[]{:S(2)}) copy-start(bf16[256,256]{1,0:T(8,128)(2,1)} %val_w.2) | copy-start | bytes 393220
  0.0 26.1 %copy-start.3 = (bf16[256,512]{1,0:T(8,128)(2,1)S(1)}, bf16[256,512]{1,0:T(8,128)(2,1)}, u32[]{:S(2)}) copy-start(bf16[256,512]{1,0:T(8,128)(2,1)} %qk_w.2) | copy-start | bytes 786436
  0.0 26.1 %copy-start.9 = (f32[256]{0:T(256)S(1)}, f32[256]{0:T(256)}, u32[]{:S(2)}) copy-start(f32[256]{0:T(256)} %param.17) | copy-start | bytes 3076
  0.0 26.1 %copy-start.10 = (f32[256]{0:T(256)S(1)}, f32[256]{0:T(256)}, u32[]{:S(2)}) copy-start(f32[256]{0:T(256)} %param.21) | copy-start | bytes 3076
  26.1 0.7 copy-start.8
  39.3 23.6 %copy-start.2 = (bf16[256,512]{1,0:T(8,128)(2,1)S(1)}, bf16[256,512]{1,0:T(8,128)(2,1)}, u32[]{:S(2)}) copy-start(bf16[256,512]{1,0:T(8,128)(2,1)} %qk_w.3) | copy-start | bytes 786436
  39.3 23.6 %copy-start.4 = (bf16[256,256]{1,0:T(8,128)(2,1)S(1)}, bf16[256,256]{1,0:T(8,128)(2,1)}, u32[]{:S(2)}) copy-start(bf16[256,256]{1,0:T(8,128)(2,1)} %val_w.3) | copy-start | bytes 393220
  39.3 23.6 %copy-start.5 = (bf16[256,256]{1,0:T(8,128)(2,1)S(1)}, bf16[256,256]{1,0:T(8,128)(2,1)}, u32[]{:S(2)}) copy-start(bf16[256,256]{1,0:T(8,128)(2,1)} %out_w.4) | copy-start | bytes 393220
  75.4 19.0 %copy-start = (bf16[256,1024]{1,0:T(8,128)(2,1)S(1)}, bf16[256,1024]{1,0:T(8,128)(2,1)}, u32[]{:S(2)}) copy-start(bf16[256,1024]{1,0:T(8,128)(2,1)} %in_w.1) | copy-start | bytes 1572868
  75.5 19.0 %copy-start.1 = (bf16[1024,256]{1,0:T(8,128)(2,1)S(1)}, bf16[1024,256]{1,0:T(8,128)(2,1)}, u32[]{:S(2)}) copy-start(bf16[1024,256]{1,0:T(8,128)(2,1)} %out_w.5) | copy-start | bytes 1572868

commit v3 on v2

--- a/solution.py
+++ b/solution.py
@@ -1,3 +1,4 @@
+import functools
 import math
 
 import jax
@@ -16,6 +17,7 @@
 GROUPS = 2
 IN_GROUP = 4
 BLOCK = 256
+CHUNK = 256
 SCALE = math.log2(math.e) / math.sqrt(HEAD)
 GELU_A = math.sqrt(2.0 / math.pi)
 GELU_B = GELU_A * 0.044715
@@ -32,25 +34,24 @@
     return jnp.dot(left, right, preferred_element_type=jnp.float32)
 
 
-def fill_ones(mixer):
-    lane = lax.broadcasted_iota(jnp.int32, (LINE, HALF), 1) // HEAD
-    for group in range(GROUPS):
-        for head in range(IN_GROUP):
-            ones = jnp.where(lane == head, 1.0, 0.0).astype(jnp.bfloat16)
-            mixer[group, head * LINE : (head + 1) * LINE, HALF:] = ones
+def dot(left, right, left_dim, right_dim):
+    return lax.dot_general(
+        left, right, (((left_dim,), (right_dim,)), ((), ())), preferred_element_type=jnp.float32
+    )
 
 
 class Line:
-    def __init__(self, load, store, gain, qk_w, val_w, out_w, mixer, probs):
+    def __init__(self, load, store, gain, qk_w, val_w, out_w, probs):
         self.load, self.store = load, store
         self.gain, self.qk_w, self.val_w, self.out_w = gain, qk_w, val_w, out_w
-        self.mixer, self.probs = mixer, probs
+        self.probs = probs
+        self.largest = {}
         self.mixed = []
 
     def project(self):
         normed = layer_norm(self.load(), self.gain[...]).astype(jnp.bfloat16)
         both = matmul(normed, self.qk_w[...])
-        self.values = matmul(normed, self.val_w[...]).astype(jnp.bfloat16)
+        self.values = dot(self.val_w[...], normed, 0, 1).astype(jnp.bfloat16)
         query = both[:, :WIDTH].astype(jnp.bfloat16).astype(jnp.float32) * SCALE
         self.query_hi = query.astype(jnp.bfloat16)
         self.query_lo = (query - self.query_hi.astype(jnp.float32)).astype(jnp.bfloat16)
@@ -60,30 +61,42 @@
         lanes = slice(group * HALF, (group + 1) * HALF)
         query = jnp.concatenate([self.query_hi[:, lanes], self.query_lo[:, lanes]], axis=1)
         keys = self.keys[:, lanes]
-        values = self.values[:, lanes]
         zero = jnp.zeros_like(keys)
         lane = lax.broadcasted_iota(jnp.int32, (LINE, HALF), 1) // HEAD
         for head in range(IN_GROUP):
-            rows = slice(head * LINE, (head + 1) * LINE)
-            self.mixer[group, rows, :HALF] = jnp.where(lane == head, values, zero)
             head_keys = jnp.where(lane == head, keys, zero)
             head_keys = jnp.concatenate([head_keys, head_keys], axis=1)
             for start in range(0, LINE, BLOCK):
-                scores = lax.dot_general(
-                    query[start : start + BLOCK],
-                    head_keys,
-                    (((1,), (1,)), ((), ())),
-                    preferred_element_type=jnp.float32,
+                here = slice(start, start + BLOCK)
+                for chunk in range(0, LINE, CHUNK):
+                    rows = slice(chunk, chunk + CHUNK)
+                    scores = dot(head_keys[rows], query[here], 1, 1)
+                    largest = jnp.max(scores, axis=0, keepdims=True)
+                    self.largest[group, head, chunk, start] = largest
+                    weights = jnp.exp2(scores - largest).astype(jnp.bfloat16)
+                    self.probs[group * IN_GROUP + head, rows, here] = weights
+
+    def mix(self, group):
+        ones = jnp.ones((16, LINE), jnp.bfloat16)
+        for head in range(IN_GROUP):
+            index = group * IN_GROUP + head
+            values = jnp.concatenate([self.values[index * HEAD : (index + 1) * HEAD], ones], axis=0)
+            chunks = range(0, LINE, CHUNK)
+            scales = [
+                jnp.concatenate(
+                    [self.largest[group, head, chunk, start] for start in range(0, LINE, BLOCK)], axis=1
                 )
-                scores = scores - jnp.max(scores, axis=-1, keepdims=True)
-                self.probs[group, start : start + BLOCK, rows] = jnp.exp2(scores).astype(jnp.bfloat16)
-
-    def mix(self, group):
-        sums = matmul(self.probs[group], self.mixer[group])
-        self.mixed.append((sums[:, :HALF] / sums[:, HALF:]).astype(jnp.bfloat16))
+                for chunk in chunks
+            ]
+            largest = functools.reduce(jnp.maximum, scales)
+            total = 0.0
+            for chunk, scale in zip(chunks, scales):
+                rows = slice(chunk, chunk + CHUNK)
+                total += matmul(values[:, rows], self.probs[index, rows]) * jnp.exp2(scale - largest)
+            self.mixed.append((total[:HEAD] / total[HEAD : HEAD + 1]).astype(jnp.bfloat16))
 
     def finish(self):
-        self.store(self.load() + matmul(jnp.concatenate(self.mixed, axis=1), self.out_w[...]))
+        self.store(self.load() + dot(jnp.concatenate(self.mixed, axis=0), self.out_w[...], 0, 0))
 
 
 def attend(lines):
@@ -101,9 +114,8 @@
 
 
 def row_kernel(
-    cells, gain, qk_w, val_w, out_w, later_gain, last_gain, out, later_out, last_out, mixer, probs, turned
+    cells, gain, qk_w, val_w, out_w, later_gain, last_gain, out, later_out, last_out, probs, turned
 ):
-    fill_ones(mixer)
     later_out[...] = later_gain[...]
     last_out[...] = last_gain[...]
 
@@ -115,7 +127,7 @@
             for lanes in range(GROUPS):
                 turned[lanes, pl.ds(j, LINE, stride=LINES), :] = done[:, lanes * HALF : (lanes + 1) * HALF]
 
-        return Line(load, store, gain, qk_w, val_w, out_w, mixer, probs)
+        return Line(load, store, gain, qk_w, val_w, out_w, probs)
 
     attend([line(j) for j in range(LINES)])
     n_row, n_col, deep = out.shape[:3]
@@ -126,8 +138,7 @@
             out[r, :, :, here] = blocks[:, r]
 
 
-def col_kernel(cells, gain, qk_w, val_w, out_w, out, mixer, probs):
-    fill_ones(mixer)
+def col_kernel(cells, gain, qk_w, val_w, out_w, out, probs):
 
     def line(m):
         def load():
@@ -144,7 +155,7 @@
         def store(done):
             out[:, m] = done.astype(jnp.bfloat16).reshape(out.shape[0], out.shape[2], WIDTH)
 
-        return Line(load, store, gain, qk_w, val_w, out_w, mixer, probs)
+        return Line(load, store, gain, qk_w, val_w, out_w, probs)
 
     attend([line(m) for m in range(LINES)])
 
@@ -157,16 +168,16 @@
     come = lax.broadcasted_iota(jnp.int32, (cells, cells), 1)
     moved = come == to % cols * deep + to // cols
     swap[...] = jnp.where(moved, 1.0, 0.0).astype(jnp.bfloat16)
+    parts = [slice(part * deep, (part + 1) * deep) for part in range(LINES)]
+    lines = [matmul(swap[...], blocks[:, :, here].reshape(cells, WIDTH)) for here in parts]
+    normed = [layer_norm(line, gain[...]).astype(jnp.bfloat16) for line in lines]
     copies = []
-    for part in range(LINES):
-        here = slice(part * deep, (part + 1) * deep)
-        line = matmul(swap[...], blocks[:, :, here].reshape(cells, WIDTH))
-        normed = layer_norm(line, gain[...]).astype(jnp.bfloat16)
+    for part, here in enumerate(parts):
         for start in range(0, cells, BLOCK):
-            pre = matmul(normed[start : start + BLOCK], in_w[...])
+            pre = matmul(normed[part][start : start + BLOCK], in_w[...])
             inner = jnp.tanh(pre * (GELU_A + GELU_B * (pre * pre)))
             hidden = (pre * (0.5 + 0.5 * inner)).astype(jnp.bfloat16)
-            result = line[start : start + BLOCK] + matmul(hidden, out_w[...])
+            result = lines[part][start : start + BLOCK] + matmul(hidden, out_w[...])
             first = part * deep + start // cols
             done[first : first + BLOCK // cols] = result.astype(jnp.bfloat16).reshape(
                 BLOCK // cols, cols, WIDTH
@@ -186,10 +197,7 @@
 
 
 def attend_scratch():
-    return [
-        pltpu.VMEM((GROUPS, IN_GROUP * LINE, WIDTH), jnp.bfloat16),
-        pltpu.VMEM((GROUPS, LINE, IN_GROUP * LINE), jnp.bfloat16),
-    ]
+    return [pltpu.VMEM((HEADS, LINE, LINE), jnp.bfloat16)]
 
 
 def row_attention(n_row, strips, gain, qk_w, val_w, out_w, *gains):

time: 101 us -> 96.5 us (0.955)
  Pallas kernels: 30.6 us -> 26.6 us
    pallas_call x1, Pallas kernels: 12.5 us -> 10.8 us  [row_attention(): pl.pallas_call(row_kernel, in_specs=[IN_VMEM] * 7, out_specs=[IN_VMEM] *...]
    pallas_call x1, Pallas kernels: 12.5 us -> 11 us  [col_attention(): pl.pallas_call(col_kernel, in_specs=[IN_VMEM] * 5, out_specs=IN_VMEM, out...]
where the time goes in v3:
time: 96.5 us; the launch traced here: 96.3 us
  blocking collectives  68.6 us (71%)
  Pallas kernels  26.6 us (28%)
    all_to_all x1, blocking collectives, per_device(): lax.all_to_all(cells, 'col', split_axis=0, concat_axis=0, tiled=True)  26.1 us
    all_to_all x1, blocking collectives, per_device(): lax.all_to_all(after_rows.reshape(-1, width), ('row', 'col'), split_axis=...  23.5 us
    all_to_all x1, blocking collectives, per_device(): lax.all_to_all(after_cols.reshape(-1, width), 'row', split_axis=0, concat...  19 us
    pallas_call x1, Pallas kernels, col_attention(): pl.pallas_call(col_kernel, in_specs=[IN_VMEM] * 5, out_specs=IN_VMEM, out...  11 us
    pallas_call x1, Pallas kernels, row_attention(): pl.pallas_call(row_kernel, in_specs=[IN_VMEM] * 7, out_specs=[IN_VMEM] *...  10.8 us
    pallas_call x1, Pallas kernels, mlp(): pl.pallas_call(mlp_kernel, in_specs=[IN_VMEM] * 4, out_specs=pl.BlockSpec...  4.91 us

profile of v3, /device:TPU:0, one launch (start us, length us, event | category | flops | bytes accessed | tf_op | source)
XLA Modules:
  0.0 96.3 jit_solution(2103444019922042412)
XLA Ops:
  0.0 0.0 copy-start.7
  0.0 0.0 copy-start.6
  0.0 0.0 copy-start.3
  0.0 0.0 copy-start.9
  0.0 0.0 copy-start.10
  0.0 26.1 %all_to_all.25 = bf16[64,32,256]{2,1,0:T(8,128)(2,1)S(1)} all-to-all(bf16[64,32,256]{2,1,0:T(8,128)(2,1)} %param.12), channel_id=1, replica_groups=mesh['row'=8,'col'=16] {'col'}, dimensions={0} | all-to-all | bytes 2097152 | tf_op jit(solution)/shard_map/all_to_all | solution.py:265
  26.1 0.0 copy-start.8
  26.1 0.0 copy-done.7
  26.1 0.0 copy-done.6
  26.1 0.0 copy-done.3
  26.1 0.0 copy-done.9
  26.1 0.0 copy-done.10
  26.1 0.6 copy-done.8
  26.8 10.8 %row_attention.1 = (bf16[8,16,16,256]{3,2,1,0:T(8,128)(2,1)S(1)}, f32[1,256]{1,0:T(1,128)S(1)}, f32[1,256]{1,0:T(1,128)S(1)}) custom-call(bf16[16,4,32,256]{3,2,1,0:T(8,128)(2,1)S(1)} %bitcast.10, f32[1,256]{1,0:T(1,128)S(1)} %bitcast.13, bf16[256,512]{1,0:T(8,128)(2,1)S(1)} %copy-done.3, bf16[256,256]{1,0:T(8,128)(2,1)S(1)} %copy-done.6, ...), custom_call_target="tpu_custom_call" | custom-call | tf_op jit(solution)/shard_map/row_attention/pallas_call | solution.py:205
  37.6 0.0 copy-start.2
  37.6 0.0 copy-start.4
  37.6 0.0 copy-start.5
  37.6 23.5 %all_to_all.26 = bf16[128,16,256]{2,1,0:T(8,128)(2,1)S(1)} all-to-all(bf16[128,16,256]{2,1,0:T(8,128)(2,1)S(1)} %bitcast.12), channel_id=1, replica_groups=mesh['row'=8,'col'=16] {'row','col'}, dimensions={0} | all-to-all | bytes 2097152 | tf_op jit(solution)/shard_map/all_to_all | solution.py:270
  61.1 0.0 copy-done.2
  61.1 0.0 copy-done.4
  61.1 0.0 copy-done.5
  61.2 11.0 %col_attention.1 = bf16[8,4,64,256]{3,2,1,0:T(8,128)(2,1)S(1)} custom-call(bf16[2048,256]{1,0:T(8,128)(2,1)S(1)} %bitcast.8, f32[1,256]{1,0:T(1,128)S(1)} %get-tuple-element.9.gain, bf16[256,512]{1,0:T(8,128)(2,1)S(1)} %copy-done.2, bf16[256,256]{1,0:T(8,128)(2,1)S(1)} %copy-done.4, bf16[256,256]{1,0:T(8,128)(2,1)S(1)} %copy-done.5), custom_call_target="tpu_custom_call" | custom-call | tf_op jit(solution)/shard_map/col_attention/pallas_call | solution.py:218
  72.1 0.0 copy-start
  72.1 0.0 copy-start.1
  72.1 19.0 %all_to_all.27 = bf16[8,256,256]{2,1,0:T(8,128)(2,1)S(1)} all-to-all(bf16[8,256,256]{2,1,0:T(8,128)(2,1)S(1)} %bitcast.9), channel_id=1, replica_groups=mesh['row'=8,'col'=16] {'row'}, dimensions={0} | all-to-all | bytes 2097152 | tf_op jit(solution)/shard_map/all_to_all | solution.py:274
  91.2 0.0 copy-done
  91.2 0.0 copy-done.1
  91.2 4.9 %mlp.1 = bf16[64,32,256]{2,1,0:T(8,128)(2,1)} custom-call(bf16[8,4,64,256]{3,2,1,0:T(8,128)(2,1)S(1)} %bitcast.11, f32[1,256]{1,0:T(1,128)S(1)} %get-tuple-element.10.gain, bf16[256,1024]{1,0:T(8,128)(2,1)S(1)} %copy-done, bf16[1024,256]{1,0:T(8,128)(2,1)S(1)} %copy-done.1), custom_call_target="tpu_custom_call" | custom-call | tf_op jit(solution)/shard_map/mlp/pallas_call | solution.py:232
Async XLA Ops:
  0.0 26.1 %copy-start.7 = (bf16[256,256]{1,0:T(8,128)(2,1)S(1)}, bf16[256,256]{1,0:T(8,128)(2,1)}, u32[]{:S(2)}) copy-start(bf16[256,256]{1,0:T(8,128)(2,1)} %out_w.3) | copy-start | bytes 393220
  0.0 26.1 %copy-start.6 = (bf16[256,256]{1,0:T(8,128)(2,1)S(1)}, bf16[256,256]{1,0:T(8,128)(2,1)}, u32[]{:S(2)}) copy-start(bf16[256,256]{1,0:T(8,128)(2,1)} %val_w.2) | copy-start | bytes 393220
  0.0 26.1 %copy-start.3 = (bf16[256,512]{1,0:T(8,128)(2,1)S(1)}, bf16[256,512]{1,0:T(8,128)(2,1)}, u32[]{:S(2)}) copy-start(bf16[256,512]{1,0:T(8,128)(2,1)} %qk_w.2) | copy-start | bytes 786436
  0.0 26.1 %copy-start.9 = (f32[256]{0:T(256)S(1)}, f32[256]{0:T(256)}, u32[]{:S(2)}) copy-start(f32[256]{0:T(256)} %param.17) | copy-start | bytes 3076
  0.0 26.1 %copy-start.10 = (f32[256]{0:T(256)S(1)}, f32[256]{0:T(256)}, u32[]{:S(2)}) copy-start(f32[256]{0:T(256)} %param.21) | copy-start | bytes 3076
  26.1 0.7 copy-start.8
  37.6 23.6 %copy-start.2 = (bf16[256,512]{1,0:T(8,128)(2,1)S(1)}, bf16[256,512]{1,0:T(8,128)(2,1)}, u32[]{:S(2)}) copy-start(bf16[256,512]{1,0:T(8,128)(2,1)} %qk_w.3) | copy-start | bytes 786436
  37.6 23.6 %copy-start.4 = (bf16[256,256]{1,0:T(8,128)(2,1)S(1)}, bf16[256,256]{1,0:T(8,128)(2,1)}, u32[]{:S(2)}) copy-start(bf16[256,256]{1,0:T(8,128)(2,1)} %val_w.3) | copy-start | bytes 393220
  37.6 23.6 %copy-start.5 = (bf16[256,256]{1,0:T(8,128)(2,1)S(1)}, bf16[256,256]{1,0:T(8,128)(2,1)}, u32[]{:S(2)}) copy-start(bf16[256,256]{1,0:T(8,128)(2,1)} %out_w.4) | copy-start | bytes 393220
  72.1 19.0 %copy-start = (bf16[256,1024]{1,0:T(8,128)(2,1)S(1)}, bf16[256,1024]{1,0:T(8,128)(2,1)}, u32[]{:S(2)}) copy-start(bf16[256,1024]{1,0:T(8,128)(2,1)} %in_w.1) | copy-start | bytes 1572868
  72.1 19.0 %copy-start.1 = (bf16[1024,256]{1,0:T(8,128)(2,1)S(1)}, bf16[1024,256]{1,0:T(8,128)(2,1)}, u32[]{:S(2)}) copy-start(bf16[1024,256]{1,0:T(8,128)(2,1)} %out_w.5) | copy-start | bytes 1572868
